TPU v7x, 512 devices: a whole 4x8x8 slice. The times are simulated.
512 devices in a mesh: stream: 32 (over z, x), cross: 16 (over y, core).
Axes of the slice: x: 4, y: 8, z: 8, core: 2. Of those that a mesh axis runs over, the one named last changes fastest.
Arguments:
- adjoint: float32 [5, 128, 16384], P(None, 'stream', 'cross'), may hold values from -6 to 6
- source: float32 [5, 128, 16384], P(None, 'stream', 'cross'), may hold values from -30 to 30
- shape_grad: float32 [5, 128, 16384], P(None, 'stream', 'cross'), may hold values from -6 to 6
- lower_band: float32 [2, 5, 128, 16384], P(None, None, 'stream', 'cross'), may hold values from -1.5 to 0.5
- upper_band: float32 [3, 5, 128, 16384], P(None, None, 'stream', 'cross'), may hold values from -6 to 2, as said below
- jacobian: float32 [5, 5], replicated, may hold values from -2.5 to 2.5
- left_vectors: float32 [5, 5], replicated, may hold values from -1 to 2
- right_vectors: float32 [5, 5], replicated, may hold values from -1 to 2
- ctrl_local: int32 [128, 16384], P('stream', 'cross'), may hold values from 0 to 16383
Outputs:
- adjoint_next: float32 [5, 128, 16384], P(None, 'stream', 'cross')
- sensitivity: float32 [524288], P(('stream', 'cross'))
Inputs may be any that keep to these rules, and one draw needn't show every extreme that they name: upper_band[0] lies in 0.5 to 2.
All inputs are finite; a program needn't handle non-finite values.
Results may differ from a plain program's by a relative error of at most 0.00029.
Values sent between devices are 32-bit elements; how exact they have to be, the bound alone decides.
A program may use at most 64 MiB of HBM per device.

v0:
```python
import jax
import jax.numpy as jnp
from jax import lax
from jax.sharding import PartitionSpec as P

NF = 5
NCTRL = 524288


dissipation = 0.25
step_scale = 0.5
epsilon = 1e-06


def with_halo(array, sides, width):
    for axis, dim in sides:
        size, length = (lax.axis_size(axis), array.shape[dim])
        up = [(i, (i + 1) % size) for i in range(size - 1)]
        down = [(j, i) for i, j in up]
        last = lax.slice_in_dim(array, length - width, length, axis=dim)
        first = lax.slice_in_dim(array, 0, width, axis=dim)
        before = lax.ppermute(last, axis, up)
        after = lax.ppermute(first, axis, down)
        array = jnp.concatenate([before, array, after], axis=dim)
    return array


def compose(earlier, later):
    return (
        later[0] * earlier[0] + later[1] * earlier[2],
        later[0] * earlier[1] + later[1] * earlier[3],
        later[2] * earlier[0] + later[3] * earlier[2],
        later[2] * earlier[1] + later[3] * earlier[3],
        later[0] * earlier[4] + later[1] * earlier[5] + later[4],
        later[2] * earlier[4] + later[3] * earlier[5] + later[5],
    )


def forward_maps(rhs_cells, first_sub, second_sub):
    unit_fill = jnp.ones_like(rhs_cells)
    zero_fill = jnp.zeros_like(rhs_cells)
    return (-first_sub, -second_sub, unit_fill, zero_fill, rhs_cells, zero_fill)


def backward_maps(rhs_cells, diag_cells, first_sup, second_sup):
    unit_fill = jnp.ones_like(rhs_cells)
    zero_fill = jnp.zeros_like(rhs_cells)
    return (
        -first_sup / diag_cells,
        -second_sup / diag_cells,
        unit_fill,
        zero_fill,
        rhs_cells / diag_cells,
        zero_fill,
    )


def line_scan(cell_maps, flipped):
    if flipped:
        cell_maps = tuple((jnp.flip(entry, 1) for entry in cell_maps))
    running = lax.associative_scan(compose, cell_maps, axis=1)
    if flipped:
        running = tuple((jnp.flip(entry, 1) for entry in running))
    return running


def solve_whole(pieces):
    rhs_cells, first_sub, second_sub, diag_cells, first_sup, second_sup = pieces
    forward = line_scan(forward_maps(rhs_cells, first_sub, second_sub), False)[4]
    return line_scan(backward_maps(forward, diag_cells, first_sup, second_sup), True)[4]


def shards(
    adjoint,
    source,
    shape_grad,
    lower_band,
    upper_band,
    jacobian,
    left_vectors,
    right_vectors,
    ctrl_local,
):
    highest = lax.Precision.HIGHEST
    contribution = jnp.sum(adjoint * shape_grad, axis=0)
    slab_size = NCTRL // lax.axis_size("stream")
    local_sums = jax.ops.segment_sum(
        contribution.ravel(), ctrl_local.ravel(), num_segments=slab_size
    )
    sensitivity = lax.psum_scatter(local_sums, "cross", scatter_dimension=0, tiled=True)
    padded = with_halo(adjoint, (("stream", 1),), 1)
    ahead_cells = padded[:, 2:, :]
    behind = padded[:, :-2, :]
    central = jnp.einsum("fg,gij->fij", jacobian, ahead_cells - behind, precision=highest)
    residual = source - 0.5 * central + dissipation * (ahead_cells - 2.0 * adjoint + behind)
    characteristic = jnp.einsum("fg,gij->fij", left_vectors, residual, precision=highest)
    packed = (
        characteristic,
        lower_band[0],
        lower_band[1],
        upper_band[0],
        upper_band[1],
        upper_band[2],
    )
    whole_lines = solve_whole(
        (
            lax.all_to_all(packed[0], "stream", split_axis=2, concat_axis=1, tiled=True),
            lax.all_to_all(packed[1], "stream", split_axis=2, concat_axis=1, tiled=True),
            lax.all_to_all(packed[2], "stream", split_axis=2, concat_axis=1, tiled=True),
            lax.all_to_all(packed[3], "stream", split_axis=2, concat_axis=1, tiled=True),
            lax.all_to_all(packed[4], "stream", split_axis=2, concat_axis=1, tiled=True),
            lax.all_to_all(packed[5], "stream", split_axis=2, concat_axis=1, tiled=True),
        )
    )
    solved = lax.all_to_all(whole_lines, "stream", split_axis=1, concat_axis=2, tiled=True)
    increment = jnp.einsum("fg,gij->fij", right_vectors, solved, precision=highest)
    squares = lax.psum(jnp.sum(increment * increment), ("stream", "cross"))
    cell_count = (
        NF * adjoint.shape[1] * adjoint.shape[2] * lax.axis_size("stream") * lax.axis_size("cross")
    )
    root_mean = jnp.sqrt(squares / cell_count + epsilon)
    adjoint_next = adjoint + step_scale * increment / root_mean
    return (adjoint_next, sensitivity)


def solution(mesh):
    in_specs = (
        P(None, "stream", "cross"),
        P(None, "stream", "cross"),
        P(None, "stream", "cross"),
        P(None, None, "stream", "cross"),
        P(None, None, "stream", "cross"),
        P(),
        P(),
        P(),
        P("stream", "cross"),
    )
    out_specs = (P(None, "stream", "cross"), P(("stream", "cross")))
    return jax.shard_map(shards, mesh=mesh, in_specs=in_specs, out_specs=out_specs, check_vma=False)
```

profile of v0, /device:TPU:1, one launch (start us, length us, event | category | flops | bytes accessed | tf_op | source)
XLA Modules:
  0.0 452.5 jit_solution(7003802689809958905)
XLA Ops:
  9.4 4.6 %collective-permute-start.1 = (f32[5,1,1024]{2,0,1:T(8,128)S(1)}, f32[5,1,1024]{2,0,1:T(8,128)S(1)}, u32[]{:S(2)}, u32[]{:S(2)}) collective-permute-start(f32[5,1,1024]{2,0,1:T(8,128)S(1)} %get-tuple-element.44), channel_id=1, source_target_pairs={{0,16},{16,32},{32,48},{48,64},{64,80},{80,96},{96,112},{112,128},... | collective-permute-start | bytes 61448 | tf_op jit(solution)/shard_map/ppermute | solution.py:22
  17.3 4.2 reshape.36
  21.5 15.5 %all-to-all-start.1 = ((f32[32,1,640]{2,1,0:T(1,128)}), f32[32,1,640]{2,1,0:T(1,128)S(1)}, u32[]{:S(2)}, u32[]{:S(2)}) async-start(f32[32,1,640]{2,1,0:T(1,128)} %reshape.36), calls=%async_computation.1 | async-start | bytes 163840 | tf_op jit(solution)/shard_map/all_to_all | solution.py:108
  42.3 3.1 bitcast_bitcast_fusion.1
  51.9 3.1 bitcast_bitcast_fusion.2
  57.9 4.3 reshape.40
  65.2 4.2 reshape.32
  69.7 9.5 %all-to-all-start.2 = ((f32[32,1,640]{2,1,0:T(1,128)}), f32[32,1,640]{2,1,0:T(1,128)S(1)}, u32[]{:S(2)}, u32[]{:S(2)}) async-start(f32[32,1,640]{2,1,0:T(1,128)} %reshape.38), calls=%async_computation.2 | async-start | bytes 163840 | tf_op jit(solution)/shard_map/all_to_all | solution.py:109
  84.8 3.9 reshape.37
  88.7 9.3 %all-to-all-start.4 = ((f32[32,1,640]{2,1,0:T(1,128)}), f32[32,1,640]{2,1,0:T(1,128)S(1)}, u32[]{:S(2)}, u32[]{:S(2)}) async-start(f32[32,1,640]{2,1,0:T(1,128)} %reshape.40), calls=%async_computation.4 | async-start | bytes 163840 | tf_op jit(solution)/shard_map/all_to_all | solution.py:111
  101.0 3.9 reshape.39
  107.1 7.0 %all-to-all-start.5 = ((f32[32,1,640]{2,1,0:T(1,128)}), f32[32,1,640]{2,1,0:T(1,128)S(1)}, u32[]{:S(2)}, u32[]{:S(2)}) async-start(f32[32,1,640]{2,1,0:T(1,128)} %reshape.42), calls=%async_computation.5 | async-start | bytes 163840 | tf_op jit(solution)/shard_map/all_to_all | solution.py:112
  114.2 3.4 bitcast_negate_fusion.2
  118.5 3.9 reshape.41
  123.1 8.5 %all-to-all-start.3 = ((f32[32,1,640]{2,1,0:T(1,128)}), f32[32,1,640]{2,1,0:T(1,128)S(1)}, u32[]{:S(2)}, u32[]{:S(2)}) async-start(f32[32,1,640]{2,1,0:T(1,128)} %reshape.32), calls=%async_computation.3 | async-start | bytes 163840 | tf_op jit(solution)/shard_map/all_to_all | solution.py:110
  131.6 3.4 bitcast_negate_fusion.1
  135.9 3.9 reshape.43
  140.6 8.8 %all-to-all-start = ((f32[32,1,640]{2,1,0:T(1,128)}), f32[32,1,640]{2,1,0:T(1,128)}, u32[]{:S(2)}, u32[]{:S(2)}) async-start(f32[32,1,640]{2,1,0:T(1,128)} %reshape.34), calls=%async_computation | async-start | bytes 163840 | tf_op jit(solution)/shard_map/all_to_all | solution.py:107
  149.4 3.4 bitcast_negate_fusion
  175.3 3.5 reshape.35
  199.3 9.3 %all-to-all-start.6 = ((f32[32,1,640]{2,1,0:T(1,128)}), f32[32,1,640]{2,1,0:T(1,128)S(1)}, u32[]{:S(2)}, u32[]{:S(2)}) async-start(f32[32,1,640]{2,1,0:T(1,128)} %reshape.44), calls=%async_computation.6 | async-start | bytes 163840 | tf_op jit(solution)/shard_map/all_to_all | solution.py:115
  208.8 22.5 %scatter_custom_fusion = f32[16384]{0:T(1024)} fusion(s32[4096]{0:T(1024)S(1)} %bitcast.124, f32[4096]{0:T(1024)S(1)} %bitcast.123, f32[]{:T(128)} %constant.9.clone.1), kind=kCustom, calls=%fused_computation.75 | custom fusion | flops 4096 | bytes 65540 | tf_op jit(solution)/shard_map/scatter-add | solution.py:87
  233.2 108.6 %all-reduce.55.cloned.1.call-done = f32[16384]{0:T(1024)} async-done(((f32[16384]{0:T(1024)}), f32[16384]{0:T(1024)}) %all-reduce.55.cloned.1.call-update) | async-done | bytes 65552
  345.3 98.7 %psum.7 = f32[]{:T(128)} all-reduce(f32[]{:T(128)} %get-tuple-element.108), channel_id=1, replica_groups=mesh['stream'=32,'cross'=16] {'stream','cross'}, use_global_device_ids=true, to_apply=%region_1.0 | all-reduce | flops 1 | bytes 8 | tf_op jit(solution)/shard_map/psum | solution.py:117
  (434 shorter events, 84.3 us)
Async XLA Ops:
  7.2 337.2 %copy-start = (f32[5,5]{1,0:T(8,128)S(1)}, f32[5,5]{1,0:T(8,128)}, u32[]{:S(2)}) copy-start(f32[5,5]{1,0:T(8,128)} %param.16) | copy-start | bytes 304
  8.1 61.3 %collective-permute-start = (f32[5,1,1024]{2,0,1:T(8,128)S(1)}, f32[5,1,1024]{2,0,1:T(8,128)S(1)}, u32[]{:S(2)}, u32[]{:S(2)}) collective-permute-start(f32[5,1,1024]{2,0,1:T(8,128)S(1)} %get-tuple-element.45), channel_id=1, source_target_pairs={{16,0},{32,16},{48,32},{64,48},{80,64},{96,80},{112,96},{128,112},... | collective-permute-start | bytes 61448 | tf_op jit(solution)/shard_map/ppermute | solution.py:23
  9.4 60.0 %collective-permute-start.1 = (f32[5,1,1024]{2,0,1:T(8,128)S(1)}, f32[5,1,1024]{2,0,1:T(8,128)S(1)}, u32[]{:S(2)}, u32[]{:S(2)}) collective-permute-start(f32[5,1,1024]{2,0,1:T(8,128)S(1)} %get-tuple-element.44), channel_id=1, source_target_pairs={{0,16},{16,32},{32,48},{48,64},{64,80},{80,96},{96,112},{112,128},... | collective-permute-start | bytes 61448 | tf_op jit(solution)/shard_map/ppermute | solution.py:22
  21.5 48.2 %all-to-all-start.1 = ((f32[32,1,640]{2,1,0:T(1,128)}), f32[32,1,640]{2,1,0:T(1,128)S(1)}, u32[]{:S(2)}, u32[]{:S(2)}) async-start(f32[32,1,640]{2,1,0:T(1,128)} %reshape.36), calls=%async_computation.1 | async-start | bytes 163840 | tf_op jit(solution)/shard_map/all_to_all | solution.py:108
  57.9 4.3 copy-start.2
  62.3 7.2 %copy-start.12 = (f32[5,4,1024]{2,1,0:T(4,128)S(1)}, f32[5,4,1024]{2,1,0:T(4,128)}, u32[]{:S(2)}) copy-start(f32[5,4,1024]{2,1,0:T(4,128)} %param.10) | copy-start | bytes 245764
  62.3 7.2 %copy-start.15 = (f32[5,5]{1,0:T(8,128)S(1)}, f32[5,5]{1,0:T(8,128)}, u32[]{:S(2)}) copy-start(f32[5,5]{1,0:T(8,128)} %param.14) | copy-start | bytes 304
  62.3 17.0 %copy-start.16 = (f32[5,5]{1,0:T(8,128)S(1)}, f32[5,5]{1,0:T(8,128)}, u32[]{:S(2)}) copy-start(f32[5,5]{1,0:T(8,128)} %param.15) | copy-start | bytes 304
  69.7 19.0 %all-to-all-start.2 = ((f32[32,1,640]{2,1,0:T(1,128)}), f32[32,1,640]{2,1,0:T(1,128)S(1)}, u32[]{:S(2)}, u32[]{:S(2)}) async-start(f32[32,1,640]{2,1,0:T(1,128)} %reshape.38), calls=%async_computation.2 | async-start | bytes 163840 | tf_op jit(solution)/shard_map/all_to_all | solution.py:109
  88.7 18.4 %all-to-all-start.4 = ((f32[32,1,640]{2,1,0:T(1,128)}), f32[32,1,640]{2,1,0:T(1,128)S(1)}, u32[]{:S(2)}, u32[]{:S(2)}) async-start(f32[32,1,640]{2,1,0:T(1,128)} %reshape.40), calls=%async_computation.4 | async-start | bytes 163840 | tf_op jit(solution)/shard_map/all_to_all | solution.py:111
  107.1 16.0 %all-to-all-start.5 = ((f32[32,1,640]{2,1,0:T(1,128)}), f32[32,1,640]{2,1,0:T(1,128)S(1)}, u32[]{:S(2)}, u32[]{:S(2)}) async-start(f32[32,1,640]{2,1,0:T(1,128)} %reshape.42), calls=%async_computation.5 | async-start | bytes 163840 | tf_op jit(solution)/shard_map/all_to_all | solution.py:112
  123.1 17.5 %all-to-all-start.3 = ((f32[32,1,640]{2,1,0:T(1,128)}), f32[32,1,640]{2,1,0:T(1,128)S(1)}, u32[]{:S(2)}, u32[]{:S(2)}) async-start(f32[32,1,640]{2,1,0:T(1,128)} %reshape.32), calls=%async_computation.3 | async-start | bytes 163840 | tf_op jit(solution)/shard_map/all_to_all | solution.py:110
  140.6 32.3 %all-to-all-start = ((f32[32,1,640]{2,1,0:T(1,128)}), f32[32,1,640]{2,1,0:T(1,128)}, u32[]{:S(2)}, u32[]{:S(2)}) async-start(f32[32,1,640]{2,1,0:T(1,128)} %reshape.34), calls=%async_computation | async-start | bytes 163840 | tf_op jit(solution)/shard_map/all_to_all | solution.py:107
  155.4 9.0 %copy-start.1 = (f32[5,4,1024]{0,1,2:T(4,128)S(1)}, f32[5,4,1024]{0,1,2:T(4,128)}, u32[]{:S(2)}) copy-start(f32[5,4,1024]{0,1,2:T(4,128)} %bitcast_negate_fusion.1) | copy-start | bytes 245764
  180.6 3.4 copy-start.6
  180.6 3.4 copy-start.7
  180.6 3.4 copy-start.8
  185.9 1.9 copy-start.9
  185.9 1.9 copy-start.10
  197.9 10.8 %copy-start.3 = (f32[5,4,1024]{2,1,0:T(4,128)S(1)}, f32[5,4,1024]{2,1,0:T(4,128)}, u32[]{:S(2)}) copy-start(f32[5,4,1024]{2,1,0:T(4,128)} %param.9) | copy-start | bytes 245764
  198.0 10.8 %copy-start.13 = (f32[5,4,1024]{2,1,0:T(4,128)S(1)}, f32[5,4,1024]{2,1,0:T(4,128)}, u32[]{:S(2)}) copy-start(f32[5,4,1024]{2,1,0:T(4,128)} %param.11) | copy-start | bytes 245764
  198.0 10.8 %copy-start.14 = (s32[4,1024]{1,0:T(4,128)S(1)}, s32[4,1024]{1,0:T(4,128)}, u32[]{:S(2)}) copy-start(s32[4,1024]{1,0:T(4,128)} %param.17) | copy-start | bytes 49156
  199.3 143.7 %all-to-all-start.6 = ((f32[32,1,640]{2,1,0:T(1,128)}), f32[32,1,640]{2,1,0:T(1,128)S(1)}, u32[]{:S(2)}, u32[]{:S(2)}) async-start(f32[32,1,640]{2,1,0:T(1,128)} %reshape.44), calls=%async_computation.6 | async-start | bytes 163840 | tf_op jit(solution)/shard_map/all_to_all | solution.py:115
  208.7 133.1 %all-reduce.55.cloned.1.call-start = ((), (), s32[]{:S(2)}) async-start(), calls=%async_computation.7 | async-start | bytes 131072
  (3 other events, 3.7 us)
Sparse Core Ops, SparseCore 0:
  231.4 110.3 all-reduce.54
where the time goes:
time: 457 us; the launch traced here: 453 us
  waiting for transfers between devices  112 us (25%)
  local copies, waits for them, and re-layouts  103 us (23%)
  blocking collectives  98.7 us (22%)
  starting transfers between devices  73.9 us (16%)
  other arithmetic  45.3 us (10%)
  between operations  17.6 us (4%)
    unnamed x2, waiting for transfers between devices  109 us
    psum x1, blocking collectives, shards(): squares = lax.psum(jnp.sum(increment * increment), ('stream', 'cross'))  98.7 us
    unnamed x66, local copies, waits for them, and re-layouts  69.2 us
    scatter-add x1, other arithmetic, shards(): jax.ops.segment_sum(contribution.ravel(), ctrl_local.ravel(), num_segment...  22.5 us
    slice x226, local copies, waits for them, and re-layouts, line_scan(): running = lax.associative_scan(compose, cell_maps, axis=1)  17.2 us
    all_to_all x1, starting transfers between devices, shards(): lax.all_to_all(packed[1], 'stream', split_axis=2, concat_axis=1, tiled=True)  15.5 us
    all_to_all x1, starting transfers between devices, shards(): lax.all_to_all(packed[2], 'stream', split_axis=2, concat_axis=1, tiled=True)  9.51 us
    all_to_all x1, starting transfers between devices, shards(): lax.all_to_all(packed[4], 'stream', split_axis=2, concat_axis=1, tiled=True)  9.33 us
  transfers between devices with their start and end apart: 10, of which 4 were waited for; matrix products, arithmetic and copies ran while one was open for 27% of the time, Pallas kernels for 0%

commit v1 on v0

v1 whole, which is shorter than its diff:
```python
import jax
import jax.numpy as jnp
from jax import lax
from jax.experimental import pallas as pl
from jax.experimental.pallas import tpu as pltpu
from jax.sharding import PartitionSpec as P

MESH = pl.DeviceIdType.MESH
NF, CELLS = 5, 5 * 128 * 16384
NS, NC = 32, 16
dissipation = 0.25
step_scale = 0.5
epsilon = 1e-06
F32 = jnp.float32


def block_of(shape):
    return lax.broadcasted_iota(jnp.int32, shape, 1) // 32


def swap_blocks(four):
    block = block_of(four[0].shape)
    low, even = block < 2, block % 2 == 0
    a0, a1, a2, a3 = four
    m0 = pltpu.roll(jnp.where(low, a2, a0), 64, 1)
    m1 = pltpu.roll(jnp.where(low, a3, a1), 64, 1)
    x0, x2 = jnp.where(low, a0, m0), jnp.where(low, m0, a2)
    x1, x3 = jnp.where(low, a1, m1), jnp.where(low, m1, a3)
    return [
        jnp.where(even, x0, pltpu.roll(x1, 32, 1)),
        jnp.where(even, pltpu.roll(x0, 96, 1), x1),
        jnp.where(even, x2, pltpu.roll(x3, 32, 1)),
        jnp.where(even, pltpu.roll(x2, 96, 1), x3),
    ]


def mat_mul(a, b):
    return (
        a[0] * b[0] + a[1] * b[2],
        a[0] * b[1] + a[1] * b[3],
        a[2] * b[0] + a[3] * b[2],
        a[2] * b[1] + a[3] * b[3],
    )


def mat_vec(a, v):
    return (a[0] * v[0] + a[1] * v[1], a[2] * v[0] + a[3] * v[1])


def kernel(
    jac, left, right, adj_h, src_h, grad_h, low_h, up_h, ctrl_h,
    out, sens,
    adj, src, grad, low, up, ctrl, halo_s, halo_r, up_s, up_r, low_s, low_r, inc_s, inc_r,
    hot_a, hot_b, sums, cross_r, sq_s, sq_r, sq2_s, sq2_r, maps, states,
    in_sem, send_sem, recv_sem,
):
    s, c = lax.axis_index("stream"), lax.axis_index("cross")

    loads = []
    for i, (a, b) in enumerate(
        ((adj_h, adj), (up_h, up), (low_h, low), (src_h, src), (grad_h, grad), (ctrl_h, ctrl))
    ):
        copy = pltpu.make_async_copy(a, b, in_sem.at[i])
        copy.start()
        loads.append(copy)

    barrier = pltpu.get_barrier_semaphore()

    def greet_stream(k, carry):
        pl.semaphore_signal(barrier, inc=1, device_id=((s + k) % NS, c), device_id_type=MESH)
        return carry

    def greet_cross(k, carry):
        pl.semaphore_signal(barrier, inc=1, device_id=(s, (c + k) % NC), device_id_type=MESH)
        return carry

    lax.fori_loop(1, NS, greet_stream, 0)
    lax.fori_loop(1, NC, greet_cross, 0)

    def remote(a, b, n, where):
        return pltpu.make_async_remote_copy(
            src_ref=a, dst_ref=b, send_sem=send_sem.at[n], recv_sem=recv_sem.at[n],
            device_id=where, device_id_type=MESH,
        )

    def to_stream(n, source, dest):
        def body(k, carry):
            t = (s + k) % NS
            remote(source(t), dest.at[s], n, (t, c)).start()
            return carry

        lax.fori_loop(1, NS, body, 0)

    def to_cross(n, source, dest):
        def body(k, carry):
            t = (c + k) % NC
            remote(source(t), dest.at[c], n, (s, t)).start()
            return carry

        lax.fori_loop(1, NC, body, 0)

    after, before = (s + 1) % NS, (s + NS - 1) % NS

    loads[0].wait()
    halo_s[0] = adj[pl.ds(3, 40, stride=4), :]
    halo_s[1] = adj[pl.ds(0, 40, stride=4), :]
    loads[1].wait()
    for k in range(3):
        cells = [up[pl.ds(k * 160 + i, 40, stride=4), :] for i in range(4)]
        for b, packed in enumerate(swap_blocks(cells)):
            for f in range(NF):
                up_s[pl.ds(b * 16 + k * 5 + f, 8, stride=64), :] = packed[f * 8 : f * 8 + 8]

    pl.semaphore_wait(barrier, NS - 1 + NC - 1)
    behind_copy = remote(halo_s.at[0], halo_r.at[0], 0, (after, c))
    ahead_copy = remote(halo_s.at[1], halo_r.at[1], 1, (before, c))
    behind_copy.start()
    ahead_copy.start()

    def rows16(ref):
        return lambda t: ref.at[pl.ds(pl.multiple_of(t * 16, 16), 16)]

    def body_up(k, carry):
        t = (s + k) % NS
        remote(
            up_s.at[pl.ds(pl.multiple_of(t * 16, 16), 16)],
            up_r.at[pl.ds(pl.multiple_of(s * 16, 16), 16)], 2, (t, c),
        ).start()
        return carry

    lax.fori_loop(1, NS, body_up, 0)
    mine = pl.ds(pl.multiple_of(s * 16, 16), 16)
    up_r[mine, :] = up_s[mine, :]

    loads[2].wait()
    for k in range(2):
        cells = [low[pl.ds(k * 160 + i, 40, stride=4), :] for i in range(4)]
        for b, packed in enumerate(swap_blocks(cells)):
            for f in range(NF):
                low_s[pl.ds(b * 16 + k * 5 + f, 8, stride=64), :] = packed[f * 8 : f * 8 + 8]
    loads[3].wait()
    behind_copy.wait()
    ahead_copy.wait()
    own = [adj[pl.ds(i, 40, stride=4), :] for i in range(4)]
    first = jnp.where(s == 0, 0.0, halo_r[0])
    last = jnp.where(s == NS - 1, 0.0, halo_r[1])
    line = [first] + own + [last]
    characteristic = []
    for i in range(4):
        difference = line[i + 2] - line[i]
        smooth = src[pl.ds(i, 40, stride=4), :] + dissipation * (
            line[i + 2] - 2.0 * line[i + 1] + line[i]
        )
        parts = [difference[g * 8 : g * 8 + 8] for g in range(NF)]
        residual = []
        for f in range(NF):
            central = jac[f, 0] * parts[0]
            for g in range(1, NF):
                central += jac[f, g] * parts[g]
            residual.append(smooth[f * 8 : f * 8 + 8] - 0.5 * central)
        fields = []
        for f in range(NF):
            value = left[f, 0] * residual[0]
            for g in range(1, NF):
                value += left[f, g] * residual[g]
            fields.append(value)
        characteristic.append(jnp.concatenate(fields, axis=0))
    for b, packed in enumerate(swap_blocks(characteristic)):
        for f in range(NF):
            low_s[pl.ds(b * 16 + 10 + f, 8, stride=64), :] = packed[f * 8 : f * 8 + 8]

    def body_low(k, carry):
        t = (s + k) % NS
        remote(
            low_s.at[pl.ds(pl.multiple_of(t * 16, 16), 16)],
            low_r.at[pl.ds(pl.multiple_of(s * 16, 16), 16)], 3, (t, c),
        ).start()
        return carry

    lax.fori_loop(1, NS, body_low, 0)
    low_r[mine, :] = low_s[mine, :]

    loads[4].wait()
    loads[5].wait()
    terms = adj[0:32] * grad[0:32]
    for f in range(1, NF):
        terms += adj[f * 32 : f * 32 + 32] * grad[f * 32 : f * 32 + 32]
    coarse = terms.astype(jnp.bfloat16).astype(F32)
    fine = terms - coarse
    where = ctrl[...]
    high_part, low_part = where // 128, where % 128
    rows = lax.broadcasted_iota(jnp.int32, (128, 128), 0)
    for r in range(32):
        at = slice(r * 128, r * 128 + 128)
        hot_a[:, at] = jnp.where(rows == high_part[r : r + 1], 1.0, 0.0).astype(jnp.bfloat16)
        hit = rows == low_part[r : r + 1]
        hot_b[0:128, at] = jnp.where(hit, coarse[r : r + 1], 0.0).astype(jnp.bfloat16)
        hot_b[128:256, at] = jnp.where(hit, fine[r : r + 1], 0.0).astype(jnp.bfloat16)
    both = lax.dot_general(
        hot_a[...], hot_b[...], (((1,), (1,)), ((), ())), preferred_element_type=F32
    )
    sums[...] = (both[:, 0:128] + both[:, 128:256]).reshape(16, 8, 128)
    to_cross(4, lambda t: sums.at[t], cross_r)
    cross_r[c] = sums[c]

    block = block_of((40, 128))

    def unpack(ref, k):
        per_x = [
            jnp.concatenate(
                [ref[pl.ds(x * 16 + k * 5 + f, 8, stride=64), :] for f in range(NF)], axis=0
            )
            for x in range(4)
        ]
        return swap_blocks(per_x)

    def moved(values, shift, edge, fill):
        return tuple(
            jnp.where(edge, value, pltpu.roll(entry, shift, 1)) for entry, value in zip(values, fill)
        )

    unit = (1.0, 0.0, 0.0, 1.0)
    none = (0.0, 0.0)

    def prefix_mats(mats, shifts, edges):
        one = mat_mul(mats, moved(mats, shifts[0], edges[0], unit))
        two = mat_mul(one, moved(one, shifts[1], edges[1], unit))
        return one, two, moved(two, shifts[0], edges[0], unit)

    def prefix_vecs(mats, one, vecs, shifts, edges):
        moved_vecs = mat_vec(mats, moved(vecs, shifts[0], edges[0], none))
        first_vecs = tuple(a + b for a, b in zip(moved_vecs, vecs))
        moved_vecs = mat_vec(one, moved(first_vecs, shifts[1], edges[1], none))
        second = tuple(a + b for a, b in zip(moved_vecs, first_vecs))
        return second, moved(second, shifts[0], edges[0], none)

    def walk(mats, vecs, order, keep):
        for n, entry in enumerate((*mats, *vecs)):
            maps[n] = entry
        state = (jnp.zeros((NF, 128), F32),) * 2
        for z in order:
            rows_z = pl.ds(z, NF, stride=8)
            states[0, rows_z, :] = state[0]
            states[1, rows_z, :] = state[1]
            if z != order[-1]:
                at_z = [maps[n, rows_z, :] for n in range(6)]
                state = tuple(a + b for a, b in zip(mat_vec(at_z[:4], state), at_z[4:]))
        spread = []
        for n in range(2):
            value = jnp.where(block == keep, states[n], 0.0)
            value = value + pltpu.roll(value, 64, 1)
            spread.append(value + pltpu.roll(value, 32, 1))
        return spread

    def entering(mats, vecs, state):
        return tuple(a + b for a, b in zip(mat_vec(mats, state), vecs))

    def arrived(n, a, b, count, where):
        copy = remote(a.at[pl.ds(0, count)], b.at[pl.ds(0, count)], n, where)
        copy.wait()

    arrived(2, up_s, up_r, (NS - 1) * 16, (after, c))
    inverse = [1.0 / d for d in unpack(up_r, 0)]
    alpha = [u * d for u, d in zip(unpack(up_r, 1), inverse)]
    beta = [u * d for u, d in zip(unpack(up_r, 2), inverse)]
    bp, bq = [None] * 4, [None] * 4
    bp[3], bq[3] = -alpha[3], -beta[3]
    bp[2], bq[2] = -alpha[2] * bp[3] - beta[2], -alpha[2] * bq[3]
    for i in (1, 0):
        bp[i] = -alpha[i] * bp[i + 1] - beta[i] * bp[i + 2]
        bq[i] = -alpha[i] * bq[i + 1] - beta[i] * bq[i + 2]
    b_shifts, b_edges = (96, 64), (block == 3, block >= 2)
    b_mats = (bp[0], bq[0], bp[1], bq[1])
    b_one, b_two, b_before = prefix_mats(b_mats, b_shifts, b_edges)

    arrived(3, low_s, low_r, (NS - 1) * 16, (after, c))
    sub1, sub2, rhs = unpack(low_r, 0), unpack(low_r, 1), unpack(low_r, 2)
    fp, fq, fr = [-sub1[0]], [-sub2[0]], [rhs[0]]
    fp.append(-sub1[1] * fp[0] - sub2[1])
    fq.append(-sub1[1] * fq[0])
    fr.append(rhs[1] - sub1[1] * fr[0])
    for i in (2, 3):
        fp.append(-sub1[i] * fp[i - 1] - sub2[i] * fp[i - 2])
        fq.append(-sub1[i] * fq[i - 1] - sub2[i] * fq[i - 2])
        fr.append(rhs[i] - sub1[i] * fr[i - 1] - sub2[i] * fr[i - 2])
    f_shifts, f_edges = (32, 64), (block == 0, block < 2)
    f_mats = (fp[3], fq[3], fp[2], fq[2])
    f_one, f_two, f_before = prefix_mats(f_mats, f_shifts, f_edges)
    f_vecs, f_vecs_before = prefix_vecs(f_mats, f_one, (fr[3], fr[2]), f_shifts, f_edges)
    state = walk(f_two, f_vecs, list(range(8)), 3)
    enter = entering(f_before, f_vecs_before, state)
    gamma = [(fp[i] * enter[0] + fq[i] * enter[1] + fr[i]) * inverse[i] for i in range(4)]

    br = [None] * 4
    br[3] = gamma[3]
    br[2] = gamma[2] - alpha[2] * br[3]
    for i in (1, 0):
        br[i] = gamma[i] - alpha[i] * br[i + 1] - beta[i] * br[i + 2]
    b_vecs, b_vecs_before = prefix_vecs(b_mats, b_one, (br[0], br[1]), b_shifts, b_edges)
    state = walk(b_two, b_vecs, list(range(7, -1, -1)), 0)
    enter = entering(b_before, b_vecs_before, state)
    solved = [bp[i] * enter[0] + bq[i] * enter[1] + br[i] for i in range(4)]

    increment = []
    squares = jnp.zeros((8, 128), F32)
    for i in range(4):
        parts = [solved[i][g * 8 : g * 8 + 8] for g in range(NF)]
        fields = []
        for f in range(NF):
            value = right[f, 0] * parts[0]
            for g in range(1, NF):
                value += right[f, g] * parts[g]
            squares += value * value
            fields.append(value)
        increment.append(jnp.concatenate(fields, axis=0))

    sq_s[...] = jnp.broadcast_to(jnp.sum(squares, axis=0, keepdims=True), (8, 128))
    one_row = pl.ds(0, 1)

    def body_sq(k, carry):
        t = (s + k) % NS
        remote(sq_s.at[one_row], sq_r.at[s, one_row], 5, (t, c)).start()
        return carry

    lax.fori_loop(1, NS, body_sq, 0)
    sq_r[s] = sq_s[...]

    for x, packed in enumerate(swap_blocks(increment)):
        for f in range(NF):
            inc_s[pl.ds(x * 8 + f, 8, stride=32), :] = packed[f * 8 : f * 8 + 8]

    def body_inc(k, carry):
        t = (s + k) % NS
        remote(
            inc_s.at[pl.ds(pl.multiple_of(t * 8, 8), 8)],
            inc_r.at[pl.ds(pl.multiple_of(s * 8, 8), 8)], 6, (t, c),
        ).start()
        return carry

    lax.fori_loop(1, NS, body_inc, 0)
    eight = pl.ds(pl.multiple_of(s * 8, 8), 8)
    inc_r[eight, :] = inc_s[eight, :]

    def rows_arrived(n, ref, count, where):
        remote(ref.at[pl.ds(0, count), 0], ref.at[pl.ds(0, count), 0], n, where).wait()

    rows_arrived(5, sq_r, NS - 1, (after, c))
    sq2_s[...] = jnp.broadcast_to(
        jnp.sum(sq_r[:, 0, :], axis=0, keepdims=True), (8, 128)
    )

    def body_sq2(k, carry):
        t = (c + k) % NC
        remote(sq2_s.at[one_row], sq2_r.at[c, one_row], 7, (s, t)).start()
        return carry

    lax.fori_loop(1, NC, body_sq2, 0)
    sq2_r[c] = sq2_s[...]

    arrived(4, sums, cross_r, NC - 1, (s, (c + 1) % NC))
    sens[...] = jnp.sum(cross_r[...], axis=0)

    arrived(6, inc_s, inc_r, (NS - 1) * 8, (after, c))
    per_b = [
        jnp.concatenate(
            [inc_r[pl.ds(b * 8 + f, 8, stride=32), :] for f in range(NF)], axis=0
        )
        for b in range(4)
    ]
    mine_inc = swap_blocks(per_b)

    rows_arrived(7, sq2_r, NC - 1, (s, (c + 1) % NC))
    total = jnp.sum(jnp.sum(sq2_r[:, 0, :], axis=0, keepdims=True), axis=1, keepdims=True)
    scale = step_scale / jnp.sqrt(total * (1.0 / CELLS) + epsilon)
    for i in range(4):
        out[pl.ds(i, 40, stride=4), :] = own[i] + mine_inc[i] * scale


def rows_of(array):
    lead = array.shape[:-2]
    array = array.reshape(*lead, 4, 8, 128)
    return jnp.swapaxes(array, -3, -2).reshape(-1, 128)


def shards(adjoint, source, shape_grad, lower_band, upper_band, jacobian, left, right, ctrl_local):
    vmem = pltpu.VMEM
    smem = pl.BlockSpec(memory_space=pltpu.SMEM)
    hbm = pl.BlockSpec(memory_space=pl.ANY)
    out, sens = pl.pallas_call(
        kernel,
        out_shape=(jax.ShapeDtypeStruct((160, 128), F32), jax.ShapeDtypeStruct((8, 128), F32)),
        in_specs=[smem] * 3 + [hbm] * 6,
        out_specs=(pl.BlockSpec(memory_space=vmem),) * 2,
        scratch_shapes=[
            vmem((160, 128), F32),
            vmem((160, 128), F32),
            vmem((160, 128), F32),
            vmem((320, 128), F32),
            vmem((480, 128), F32),
            vmem((32, 128), jnp.int32),
            vmem((2, 40, 128), F32),
            vmem((2, 40, 128), F32),
            vmem((512, 128), F32),
            vmem((512, 128), F32),
            vmem((512, 128), F32),
            vmem((512, 128), F32),
            vmem((256, 128), F32),
            vmem((256, 128), F32),
            vmem((128, 4096), jnp.bfloat16),
            vmem((256, 4096), jnp.bfloat16),
            vmem((16, 8, 128), F32),
            vmem((16, 8, 128), F32),
            vmem((8, 128), F32),
            vmem((32, 8, 128), F32),
            vmem((8, 128), F32),
            vmem((16, 8, 128), F32),
            vmem((6, 40, 128), F32),
            vmem((2, 40, 128), F32),
            pltpu.SemaphoreType.DMA((6,)),
            pltpu.SemaphoreType.DMA((8,)),
            pltpu.SemaphoreType.DMA((8,)),
        ],
        compiler_params=pltpu.CompilerParams(
            collective_id=0, has_side_effects=True, vmem_limit_bytes=40 * 2**20
        ),
    )(
        jacobian, left, right,
        rows_of(adjoint), rows_of(source), rows_of(shape_grad), rows_of(lower_band),
        rows_of(upper_band), rows_of(ctrl_local),
    )
    adjoint_next = jnp.swapaxes(out.reshape(NF, 8, 4, 128), 1, 2).reshape(NF, 4, 1024)
    return adjoint_next, sens.reshape(1024)


def solution(mesh):
    cells = P(None, "stream", "cross")
    bands = P(None, None, "stream", "cross")
    in_specs = (cells, cells, cells, bands, bands, P(), P(), P(), P("stream", "cross"))
    out_specs = (cells, P(("stream", "cross")))
    return jax.shard_map(shards, mesh=mesh, in_specs=in_specs, out_specs=out_specs, check_vma=False)
```

time: 457 us -> 54.1 us (0.12)
  waiting for transfers between devices: 112 us -> 0 us
  blocking collectives: 98.7 us -> 0 us
  local copies, waits for them, and re-layouts: 103 us -> 7.84 us
  starting transfers between devices: 73.9 us -> 0 us
  other arithmetic: 45.3 us -> 0 us
  Pallas kernels: 0 us -> 45.2 us
  between operations: 17.6 us -> 0.67 us
    unnamed x2 -> x0, waiting for transfers between devices: 109 us -> none
    psum x1 -> x0, blocking collectives: 98.7 us -> none  [shards(): squares = lax.psum(jnp.sum(increment * increment), ('stream', 'cross'))]
    all_to_all x7 -> x0, starting transfers between devices: 68 us -> none  [the longest x1 15.5 us: shards(): lax.all_to_all(packed[1], 'stream', split_axis=2, concat_axis=1, tiled=True)]
    unnamed x66 -> x20, local copies, waits for them, and re-layouts: 69.2 us -> 7.84 us
    pallas_call x0 -> x1, Pallas kernels: none -> 45.2 us  [shards(): pl.pallas_call(kernel, out_shape=(jax.ShapeDtypeStruct((160, 128), F32),...]
    scatter-add x1 -> x0, other arithmetic: 22.5 us -> none  [shards(): jax.ops.segment_sum(contribution.ravel(), ctrl_local.ravel(), num_segment...]
    slice x229 -> x0, local copies, waits for them, and re-layouts: 18.2 us -> none  [the longest x226 17.2 us: line_scan(): running = lax.associative_scan(compose, cell_maps, axis=1)]
    neg x4 -> x0, other arithmetic: 12.2 us -> none  [the longest x2 5.44 us: forward_maps(): return (-first_sub, -second_sub, unit_fill, zero_fill, rhs_cells, zero_fill)]
  transfers between devices with their start and end apart: 10 -> 0, of which waited for: 4 -> 0; matrix products, arithmetic and copies ran while one was open for 27% -> 0% of each run, Pallas kernels for 0% -> 0%
where the time goes in v1:
time: 54.1 us; the launch traced here: 53.7 us
  Pallas kernels  45.2 us (84%)
  local copies, waits for them, and re-layouts  7.84 us (14%)
  between operations  0.67 us (1%)
    pallas_call x1, Pallas kernels, shards(): pl.pallas_call(kernel, out_shape=(jax.ShapeDtypeStruct((160, 128), F32),...  45.2 us
    unnamed x20, local copies, waits for them, and re-layouts  7.84 us

profile of v1, /device:TPU:1, one launch (start us, length us, event | category | flops | bytes accessed | tf_op | source)
XLA Modules:
  0.0 53.7 jit_solution(11118417664578378473)
XLA Ops:
  0.6 0.0 copy-start.7
  0.6 0.0 copy-start.6
  0.7 0.7 %copy-done.7 = f32[5,5]{1,0:T(8,128)S(1)} copy-done((f32[5,5]{1,0:T(8,128)S(1)}, f32[5,5]{1,0:T(8,128)}, u32[]{:S(2)}) %copy-start.7) | copy-done | bytes 124
  1.3 0.0 copy-done.6
  1.3 0.0 copy-start
  1.3 0.9 %copy-done = f32[3,5,4,1024]{3,2,1,0:T(4,128)S(1)} copy-done((f32[3,5,4,1024]{3,2,1,0:T(4,128)S(1)}, f32[3,5,4,1024]{3,2,1,0:T(4,128)}, u32[]{:S(2)}) %copy-start) | copy-done | bytes 245784
  2.3 0.0 copy-start.1
  2.3 0.9 %copy-done.1 = f32[2,5,4,1024]{3,2,1,0:T(4,128)S(1)} copy-done((f32[2,5,4,1024]{3,2,1,0:T(4,128)S(1)}, f32[2,5,4,1024]{3,2,1,0:T(4,128)}, u32[]{:S(2)}) %copy-start.1) | copy-done | bytes 163864
  3.2 0.0 copy-start.2
  3.2 0.9 %copy-done.2 = f32[5,4,1024]{2,1,0:T(4,128)S(1)} copy-done((f32[5,4,1024]{2,1,0:T(4,128)S(1)}, f32[5,4,1024]{2,1,0:T(4,128)}, u32[]{:S(2)}) %copy-start.2) | copy-done | bytes 81944
  4.1 0.0 copy-start.3
  4.1 0.9 %copy-done.3 = f32[5,4,1024]{2,1,0:T(4,128)S(1)} copy-done((f32[5,4,1024]{2,1,0:T(4,128)S(1)}, f32[5,4,1024]{2,1,0:T(4,128)}, u32[]{:S(2)}) %copy-start.3) | copy-done | bytes 81944
  5.0 0.0 copy-start.4
  5.0 0.9 %copy-done.4 = f32[5,4,1024]{2,1,0:T(4,128)S(1)} copy-done((f32[5,4,1024]{2,1,0:T(4,128)S(1)}, f32[5,4,1024]{2,1,0:T(4,128)}, u32[]{:S(2)}) %copy-start.4) | copy-done | bytes 81944
  5.9 0.0 copy-start.5
  5.9 0.7 %copy-done.5 = s32[4,1024]{1,0:T(4,128)S(1)} copy-done((s32[4,1024]{1,0:T(4,128)S(1)}, s32[4,1024]{1,0:T(4,128)}, u32[]{:S(2)}) %copy-start.5) | copy-done | bytes 16408
  6.6 0.0 copy-start.8
  6.6 0.7 %copy-done.8 = f32[5,5]{1,0:T(8,128)S(1)} copy-done((f32[5,5]{1,0:T(8,128)S(1)}, f32[5,5]{1,0:T(8,128)}, u32[]{:S(2)}) %copy-start.8) | copy-done | bytes 124
  7.3 45.2 %shard_map.104 = (f32[160,128]{1,0:T(8,128)S(1)}, f32[8,128]{1,0:T(8,128)S(1)}) custom-call(f32[5,5]{1,0:T(8,128)S(1)} %copy-done.6, f32[5,5]{1,0:T(8,128)S(1)} %copy-done.7, f32[5,5]{1,0:T(8,128)S(1)} %copy-done.8, f32[160,128]{1,0:T(8,128)S(1)} %bitcast.39, f32[160,128]{1,0:T(8,128)S(1)} %bitcast.40, f32[160,128]{1,0:T(8,128)S(1)} %bitcast.41, ...), custom_call_target="tpu_custom_call" | custom-call | tf_op jit(solution)/shard_map/pallas_call | solution.py:389
  52.5 0.6 %copy.20 = f32[5,4,1024]{2,1,0:T(4,128)} copy(f32[5,4,1024]{2,1,0:T(4,128)S(1)} %bitcast.38) | data formatting | bytes 163840
  53.1 0.6 %copy.21 = f32[1024]{0:T(1024)} copy(f32[1024]{0:T(1024)S(1)} %bitcast.43) | data formatting | bytes 8192
Async XLA Ops:
  0.6 0.7 %copy-start.7 = (f32[5,5]{1,0:T(8,128)S(1)}, f32[5,5]{1,0:T(8,128)}, u32[]{:S(2)}) copy-start(f32[5,5]{1,0:T(8,128)} %left.1) | copy-start | bytes 304
  0.6 0.7 %copy-start.6 = (f32[5,5]{1,0:T(8,128)S(1)}, f32[5,5]{1,0:T(8,128)}, u32[]{:S(2)}) copy-start(f32[5,5]{1,0:T(8,128)} %jac.1) | copy-start | bytes 304
  1.3 0.9 %copy-start = (f32[3,5,4,1024]{3,2,1,0:T(4,128)S(1)}, f32[3,5,4,1024]{3,2,1,0:T(4,128)}, u32[]{:S(2)}) copy-start(f32[3,5,4,1024]{3,2,1,0:T(4,128)} %param.13) | copy-start | bytes 737284
  2.3 0.9 %copy-start.1 = (f32[2,5,4,1024]{3,2,1,0:T(4,128)S(1)}, f32[2,5,4,1024]{3,2,1,0:T(4,128)}, u32[]{:S(2)}) copy-start(f32[2,5,4,1024]{3,2,1,0:T(4,128)} %param.12) | copy-start | bytes 491524
  3.2 0.9 %copy-start.2 = (f32[5,4,1024]{2,1,0:T(4,128)S(1)}, f32[5,4,1024]{2,1,0:T(4,128)}, u32[]{:S(2)}) copy-start(f32[5,4,1024]{2,1,0:T(4,128)} %param.9) | copy-start | bytes 245764
  4.1 0.9 %copy-start.3 = (f32[5,4,1024]{2,1,0:T(4,128)S(1)}, f32[5,4,1024]{2,1,0:T(4,128)}, u32[]{:S(2)}) copy-start(f32[5,4,1024]{2,1,0:T(4,128)} %param.10) | copy-start | bytes 245764
  5.0 0.9 %copy-start.4 = (f32[5,4,1024]{2,1,0:T(4,128)S(1)}, f32[5,4,1024]{2,1,0:T(4,128)}, u32[]{:S(2)}) copy-start(f32[5,4,1024]{2,1,0:T(4,128)} %param.11) | copy-start | bytes 245764
  5.9 0.7 %copy-start.5 = (s32[4,1024]{1,0:T(4,128)S(1)}, s32[4,1024]{1,0:T(4,128)}, u32[]{:S(2)}) copy-start(s32[4,1024]{1,0:T(4,128)} %param.17) | copy-start | bytes 49156
  6.6 0.7 %copy-start.8 = (f32[5,5]{1,0:T(8,128)S(1)}, f32[5,5]{1,0:T(8,128)}, u32[]{:S(2)}) copy-start(f32[5,5]{1,0:T(8,128)} %right.1) | copy-start | bytes 304

commit v2 on v1

--- a/solution.py
+++ b/solution.py
@@ -48,34 +48,46 @@
 
 
 def kernel(
-    jac, left, right, adj_h, src_h, grad_h, low_h, up_h, ctrl_h,
+    jac_h, left_h, right_h, adj_h, src_h, grad_h, low_h, up_h, ctrl_h,
     out, sens,
-    adj, src, grad, low, up, ctrl, halo_s, halo_r, up_s, up_r, low_s, low_r, inc_s, inc_r,
+    jac, left, right, adj, src, grad, low, up, ctrl, halo_s, halo_r, up_s, up_r, low_s, low_r, inc_s, inc_r,
     hot_a, hot_b, sums, cross_r, sq_s, sq_r, sq2_s, sq2_r, maps, states,
     in_sem, send_sem, recv_sem,
 ):
     s, c = lax.axis_index("stream"), lax.axis_index("cross")
 
+    def peer(k):
+        m, n = k // 4, k % 4
+        z = (s // 4 + 4 + (m + 1) // 2 * (1 - 2 * (m % 2))) % 8
+        x = (s % 4 + 2 + (n + 1) // 2 * (1 - 2 * (n % 2))) % 4
+        return z * 4 + x
+
+    def cross_peer(k):
+        m, n = k // 2, k % 2
+        y = (c // 2 + 4 + (m + 1) // 2 * (1 - 2 * (m % 2))) % 8
+        return y * 2 + (c + n + 1) % 2
+
+    barrier = pltpu.get_barrier_semaphore()
+
+    def greet_stream(k, carry):
+        pl.semaphore_signal(barrier, inc=1, device_id=(peer(k), c), device_id_type=MESH)
+        return carry
+
+    def greet_cross(k, carry):
+        pl.semaphore_signal(barrier, inc=1, device_id=(s, cross_peer(k)), device_id_type=MESH)
+        return carry
+
+    lax.fori_loop(0, NS - 1, greet_stream, 0)
+    lax.fori_loop(0, NC - 1, greet_cross, 0)
+
     loads = []
     for i, (a, b) in enumerate(
-        ((adj_h, adj), (up_h, up), (low_h, low), (src_h, src), (grad_h, grad), (ctrl_h, ctrl))
+        ((adj_h, adj), (up_h, up), (low_h, low), (src_h, src), (grad_h, grad), (ctrl_h, ctrl),
+         (jac_h, jac), (left_h, left), (right_h, right))
     ):
         copy = pltpu.make_async_copy(a, b, in_sem.at[i])
         copy.start()
         loads.append(copy)
-
-    barrier = pltpu.get_barrier_semaphore()
-
-    def greet_stream(k, carry):
-        pl.semaphore_signal(barrier, inc=1, device_id=((s + k) % NS, c), device_id_type=MESH)
-        return carry
-
-    def greet_cross(k, carry):
-        pl.semaphore_signal(barrier, inc=1, device_id=(s, (c + k) % NC), device_id_type=MESH)
-        return carry
-
-    lax.fori_loop(1, NS, greet_stream, 0)
-    lax.fori_loop(1, NC, greet_cross, 0)
 
     def remote(a, b, n, where):
         return pltpu.make_async_remote_copy(
@@ -83,22 +95,15 @@
             device_id=where, device_id_type=MESH,
         )
 
-    def to_stream(n, source, dest):
-        def body(k, carry):
-            t = (s + k) % NS
-            remote(source(t), dest.at[s], n, (t, c)).start()
-            return carry
-
-        lax.fori_loop(1, NS, body, 0)
-
     def to_cross(n, source, dest):
         def body(k, carry):
-            t = (c + k) % NC
+            t = cross_peer(k)
             remote(source(t), dest.at[c], n, (s, t)).start()
             return carry
 
-        lax.fori_loop(1, NC, body, 0)
-
+        lax.fori_loop(0, NC - 1, body, 0)
+
+    sent = []
     after, before = (s + 1) % NS, (s + NS - 1) % NS
 
     loads[0].wait()
@@ -121,14 +126,14 @@
         return lambda t: ref.at[pl.ds(pl.multiple_of(t * 16, 16), 16)]
 
     def body_up(k, carry):
-        t = (s + k) % NS
+        t = peer(k)
         remote(
-            up_s.at[pl.ds(pl.multiple_of(t * 16, 16), 16)],
-            up_r.at[pl.ds(pl.multiple_of(s * 16, 16), 16)], 2, (t, c),
+            up_s.at[pl.ds(pl.multiple_of(t * 16, 16), 15)],
+            up_r.at[pl.ds(pl.multiple_of(s * 16, 16), 15)], 2, (t, c),
         ).start()
         return carry
 
-    lax.fori_loop(1, NS, body_up, 0)
+    lax.fori_loop(0, NS - 1, body_up, 0)
     mine = pl.ds(pl.multiple_of(s * 16, 16), 16)
     up_r[mine, :] = up_s[mine, :]
 
@@ -138,9 +143,11 @@
         for b, packed in enumerate(swap_blocks(cells)):
             for f in range(NF):
                 low_s[pl.ds(b * 16 + k * 5 + f, 8, stride=64), :] = packed[f * 8 : f * 8 + 8]
-    loads[3].wait()
-    behind_copy.wait()
-    ahead_copy.wait()
+    for n in (3, 6, 7, 8):
+        loads[n].wait()
+    behind_copy.wait_recv()
+    ahead_copy.wait_recv()
+    sent += [behind_copy, ahead_copy]
     own = [adj[pl.ds(i, 40, stride=4), :] for i in range(4)]
     first = jnp.where(s == 0, 0.0, halo_r[0])
     last = jnp.where(s == NS - 1, 0.0, halo_r[1])
@@ -170,14 +177,14 @@
             low_s[pl.ds(b * 16 + 10 + f, 8, stride=64), :] = packed[f * 8 : f * 8 + 8]
 
     def body_low(k, carry):
-        t = (s + k) % NS
+        t = peer(k)
         remote(
-            low_s.at[pl.ds(pl.multiple_of(t * 16, 16), 16)],
-            low_r.at[pl.ds(pl.multiple_of(s * 16, 16), 16)], 3, (t, c),
+            low_s.at[pl.ds(pl.multiple_of(t * 16, 16), 15)],
+            low_r.at[pl.ds(pl.multiple_of(s * 16, 16), 15)], 3, (t, c),
         ).start()
         return carry
 
-    lax.fori_loop(1, NS, body_low, 0)
+    lax.fori_loop(0, NS - 1, body_low, 0)
     low_r[mine, :] = low_s[mine, :]
 
     loads[4].wait()
@@ -257,9 +264,10 @@
 
     def arrived(n, a, b, count, where):
         copy = remote(a.at[pl.ds(0, count)], b.at[pl.ds(0, count)], n, where)
-        copy.wait()
-
-    arrived(2, up_s, up_r, (NS - 1) * 16, (after, c))
+        copy.wait_recv()
+        sent.append(copy)
+
+    arrived(2, up_s, up_r, (NS - 1) * 15, (after, c))
     inverse = [1.0 / d for d in unpack(up_r, 0)]
     alpha = [u * d for u, d in zip(unpack(up_r, 1), inverse)]
     beta = [u * d for u, d in zip(unpack(up_r, 2), inverse)]
@@ -273,7 +281,7 @@
     b_mats = (bp[0], bq[0], bp[1], bq[1])
     b_one, b_two, b_before = prefix_mats(b_mats, b_shifts, b_edges)
 
-    arrived(3, low_s, low_r, (NS - 1) * 16, (after, c))
+    arrived(3, low_s, low_r, (NS - 1) * 15, (after, c))
     sub1, sub2, rhs = unpack(low_r, 0), unpack(low_r, 1), unpack(low_r, 2)
     fp, fq, fr = [-sub1[0]], [-sub2[0]], [rhs[0]]
     fp.append(-sub1[1] * fp[0] - sub2[1])
@@ -318,11 +326,11 @@
     one_row = pl.ds(0, 1)
 
     def body_sq(k, carry):
-        t = (s + k) % NS
+        t = peer(k)
         remote(sq_s.at[one_row], sq_r.at[s, one_row], 5, (t, c)).start()
         return carry
 
-    lax.fori_loop(1, NS, body_sq, 0)
+    lax.fori_loop(0, NS - 1, body_sq, 0)
     sq_r[s] = sq_s[...]
 
     for x, packed in enumerate(swap_blocks(increment)):
@@ -330,19 +338,21 @@
             inc_s[pl.ds(x * 8 + f, 8, stride=32), :] = packed[f * 8 : f * 8 + 8]
 
     def body_inc(k, carry):
-        t = (s + k) % NS
+        t = peer(k)
         remote(
             inc_s.at[pl.ds(pl.multiple_of(t * 8, 8), 8)],
             inc_r.at[pl.ds(pl.multiple_of(s * 8, 8), 8)], 6, (t, c),
         ).start()
         return carry
 
-    lax.fori_loop(1, NS, body_inc, 0)
+    lax.fori_loop(0, NS - 1, body_inc, 0)
     eight = pl.ds(pl.multiple_of(s * 8, 8), 8)
     inc_r[eight, :] = inc_s[eight, :]
 
     def rows_arrived(n, ref, count, where):
-        remote(ref.at[pl.ds(0, count), 0], ref.at[pl.ds(0, count), 0], n, where).wait()
+        copy = remote(ref.at[pl.ds(0, count), 0], ref.at[pl.ds(0, count), 0], n, where)
+        copy.wait_recv()
+        sent.append(copy)
 
     rows_arrived(5, sq_r, NS - 1, (after, c))
     sq2_s[...] = jnp.broadcast_to(
@@ -350,11 +360,11 @@
     )
 
     def body_sq2(k, carry):
-        t = (c + k) % NC
+        t = cross_peer(k)
         remote(sq2_s.at[one_row], sq2_r.at[c, one_row], 7, (s, t)).start()
         return carry
 
-    lax.fori_loop(1, NC, body_sq2, 0)
+    lax.fori_loop(0, NC - 1, body_sq2, 0)
     sq2_r[c] = sq2_s[...]
 
     arrived(4, sums, cross_r, NC - 1, (s, (c + 1) % NC))
@@ -374,6 +384,8 @@
     scale = step_scale / jnp.sqrt(total * (1.0 / CELLS) + epsilon)
     for i in range(4):
         out[pl.ds(i, 40, stride=4), :] = own[i] + mine_inc[i] * scale
+    for copy in sent:
+        copy.wait_send()
 
 
 def rows_of(array):
@@ -384,14 +396,16 @@
 
 def shards(adjoint, source, shape_grad, lower_band, upper_band, jacobian, left, right, ctrl_local):
     vmem = pltpu.VMEM
-    smem = pl.BlockSpec(memory_space=pltpu.SMEM)
     hbm = pl.BlockSpec(memory_space=pl.ANY)
     out, sens = pl.pallas_call(
         kernel,
         out_shape=(jax.ShapeDtypeStruct((160, 128), F32), jax.ShapeDtypeStruct((8, 128), F32)),
-        in_specs=[smem] * 3 + [hbm] * 6,
+        in_specs=[hbm] * 9,
         out_specs=(pl.BlockSpec(memory_space=vmem),) * 2,
         scratch_shapes=[
+            pltpu.SMEM((NF, NF), F32),
+            pltpu.SMEM((NF, NF), F32),
+            pltpu.SMEM((NF, NF), F32),
             vmem((160, 128), F32),
             vmem((160, 128), F32),
             vmem((160, 128), F32),
@@ -416,12 +430,12 @@
             vmem((16, 8, 128), F32),
             vmem((6, 40, 128), F32),
             vmem((2, 40, 128), F32),
-            pltpu.SemaphoreType.DMA((6,)),
+            pltpu.SemaphoreType.DMA((9,)),
             pltpu.SemaphoreType.DMA((8,)),
             pltpu.SemaphoreType.DMA((8,)),
         ],
         compiler_params=pltpu.CompilerParams(
-            collective_id=0, has_side_effects=True, vmem_limit_bytes=40 * 2**20
+            collective_id=0, has_side_effects=True, vmem_limit_bytes=60 * 2**20
         ),
     )(
         jacobian, left, right,

time: 54.1 us -> 46 us (0.85)
  local copies, waits for them, and re-layouts: 7.84 us -> 2.13 us
  Pallas kernels: 45.2 us -> 43.1 us
    unnamed x20 -> x4, local copies, waits for them, and re-layouts: 7.84 us -> 2.13 us
    pallas_call x1, Pallas kernels: 45.2 us -> 43.1 us  [shards(): pl.pallas_call(kernel, out_shape=(jax.ShapeDtypeStruct((160, 128), F32),...]
where the time goes in v2:
time: 46 us; the launch traced here: 45.9 us
  Pallas kernels  43.1 us (94%)
  local copies, waits for them, and re-layouts  2.13 us (5%)
  between operations  0.65 us (1%)
    pallas_call x1, Pallas kernels, shards(): pl.pallas_call(kernel, out_shape=(jax.ShapeDtypeStruct((160, 128), F32),...  43.1 us
    unnamed x4, local copies, waits for them, and re-layouts  2.13 us

profile of v2, /device:TPU:1, one launch (start us, length us, event | category | flops | bytes accessed | tf_op | source)
XLA Modules:
  0.0 45.9 jit_solution(10962037590737866182)
XLA Ops:
  0.6 43.1 %shard_map.104 = (f32[160,128]{1,0:T(8,128)}, f32[8,128]{1,0:T(8,128)}) custom-call(f32[5,5]{1,0:T(8,128)} %jac_h.1, f32[5,5]{1,0:T(8,128)} %left_h.1, f32[5,5]{1,0:T(8,128)} %right_h.1, f32[160,128]{1,0:T(8,128)} %bitcast.39, f32[160,128]{1,0:T(8,128)} %bitcast.40, f32[160,128]{1,0:T(8,128)} %bitcast.41, f32[320,128]{1,0:T(8,128)} %bitcast.37, ...), custom_call_target="tpu_custom_call" | custom-call | tf_op jit(solution)/shard_map/pallas_call | solution.py:400
  43.7 0.0 copy-start
  43.7 1.5 %copy.20 = f32[5,4,1024]{2,1,0:T(4,128)} copy(f32[5,4,1024]{2,1,0:T(4,128)} %bitcast.38) | data formatting | bytes 163840
  45.3 0.0 copy-done
  45.3 0.6 %copy.21 = f32[1024]{0:T(1024)} copy(f32[1024]{0:T(1024)S(1)} %bitcast.43) | data formatting | bytes 8192
Async XLA Ops:
  43.7 1.5 %copy-start = (f32[8,128]{1,0:T(8,128)S(1)}, f32[8,128]{1,0:T(8,128)}, u32[]{:S(2)}) copy-start(f32[8,128]{1,0:T(8,128)} %get-tuple-element.5) | copy-start | bytes 12292

commit v3 on v2

--- a/solution.py
+++ b/solution.py
@@ -50,7 +50,7 @@
 def kernel(
     jac_h, left_h, right_h, adj_h, src_h, grad_h, low_h, up_h, ctrl_h,
     out, sens,
-    jac, left, right, adj, src, grad, low, up, ctrl, halo_s, halo_r, up_s, up_r, low_s, low_r, inc_s, inc_r,
+    jac, left, right, adj, src, grad, low, up, ctrl, next_s, next_r, last_s, last_r, up_s, up_r, low_s, low_r, inc_s, inc_r,
     hot_a, hot_b, sums, cross_r, sq_s, sq_r, sq2_s, sq2_r, maps, states,
     in_sem, send_sem, recv_sem,
 ):
@@ -106,86 +106,80 @@
     sent = []
     after, before = (s + 1) % NS, (s + NS - 1) % NS
 
+    def cell(ref, k, i):
+        return ref[pl.ds(k * 160 + i, 40, stride=4), :]
+
+    def pack(ref, k, four):
+        for b, packed in enumerate(swap_blocks(four)):
+            for f in range(NF):
+                ref[pl.ds(b * 16 + k + f, 8, stride=64), :] = packed[f * 8 : f * 8 + 8]
+
+    def mixed(matrix, array):
+        parts = [array[g * 8 : g * 8 + 8] for g in range(NF)]
+        rows = []
+        for f in range(NF):
+            value = matrix[f, 0] * parts[0]
+            for g in range(1, NF):
+                value += matrix[f, g] * parts[g]
+            rows.append(value)
+        return jnp.concatenate(rows, axis=0)
+
     loads[0].wait()
-    halo_s[0] = adj[pl.ds(3, 40, stride=4), :]
-    halo_s[1] = adj[pl.ds(0, 40, stride=4), :]
+    own = [cell(adj, 0, i) for i in range(4)]
     loads[1].wait()
-    for k in range(3):
-        cells = [up[pl.ds(k * 160 + i, 40, stride=4), :] for i in range(4)]
-        for b, packed in enumerate(swap_blocks(cells)):
-            for f in range(NF):
-                up_s[pl.ds(b * 16 + k * 5 + f, 8, stride=64), :] = packed[f * 8 : f * 8 + 8]
+    diag = [cell(up, 0, i) for i in range(4)]
+    next_s[0:40] = own[3]
+    next_s[40:80] = diag[3]
+    next_s[80:120] = diag[2]
+    last_s[...] = own[0]
+    inverse = [1.0 / d for d in diag]
+    for k in (1, 2):
+        pack(up_s, k * 5 - 5, [cell(up, k, i) * inverse[i] for i in range(4)])
+    loads[2].wait()
+    sub1 = [cell(low, 0, i) * inverse[i] for i in range(4)]
+    sub2 = [cell(low, 1, i) * inverse[i] for i in range(4)]
+    pack(
+        up_s, 10, [sub1[1] * diag[0], sub1[2] * diag[1], sub1[3] * diag[2], sub2[2] * diag[0]]
+    )
 
     pl.semaphore_wait(barrier, NS - 1 + NC - 1)
-    behind_copy = remote(halo_s.at[0], halo_r.at[0], 0, (after, c))
-    ahead_copy = remote(halo_s.at[1], halo_r.at[1], 1, (before, c))
+    behind_copy = remote(next_s, next_r, 0, (after, c))
+    ahead_copy = remote(last_s, last_r, 1, (before, c))
     behind_copy.start()
     ahead_copy.start()
 
-    def rows16(ref):
-        return lambda t: ref.at[pl.ds(pl.multiple_of(t * 16, 16), 16)]
-
-    def body_up(k, carry):
-        t = peer(k)
-        remote(
-            up_s.at[pl.ds(pl.multiple_of(t * 16, 16), 15)],
-            up_r.at[pl.ds(pl.multiple_of(s * 16, 16), 15)], 2, (t, c),
-        ).start()
-        return carry
-
-    lax.fori_loop(0, NS - 1, body_up, 0)
-    mine = pl.ds(pl.multiple_of(s * 16, 16), 16)
-    up_r[mine, :] = up_s[mine, :]
-
-    loads[2].wait()
-    for k in range(2):
-        cells = [low[pl.ds(k * 160 + i, 40, stride=4), :] for i in range(4)]
-        for b, packed in enumerate(swap_blocks(cells)):
-            for f in range(NF):
-                low_s[pl.ds(b * 16 + k * 5 + f, 8, stride=64), :] = packed[f * 8 : f * 8 + 8]
+    def to_owners(n, source, dest, rows):
+        def body(k, carry):
+            t = peer(k)
+            remote(
+                source.at[pl.ds(pl.multiple_of(t * 16, 16), rows)],
+                dest.at[pl.ds(pl.multiple_of(s * 16, 16), rows)], n, (t, c),
+            ).start()
+            return carry
+
+        lax.fori_loop(0, NS - 1, body, 0)
+        mine = pl.ds(pl.multiple_of(s * 16, 16), 16)
+        dest[mine, :] = source[mine, :]
+
+    to_owners(2, up_s, up_r, 15)
+
     for n in (3, 6, 7, 8):
         loads[n].wait()
     behind_copy.wait_recv()
     ahead_copy.wait_recv()
     sent += [behind_copy, ahead_copy]
-    own = [adj[pl.ds(i, 40, stride=4), :] for i in range(4)]
-    first = jnp.where(s == 0, 0.0, halo_r[0])
-    last = jnp.where(s == NS - 1, 0.0, halo_r[1])
+    first = jnp.where(s == 0, 0.0, next_r[0:40])
+    last = jnp.where(s == NS - 1, 0.0, last_r[...])
+    diag1, diag2 = next_r[40:80], next_r[80:120]
     line = [first] + own + [last]
-    characteristic = []
+    rhs = []
     for i in range(4):
-        difference = line[i + 2] - line[i]
-        smooth = src[pl.ds(i, 40, stride=4), :] + dissipation * (
-            line[i + 2] - 2.0 * line[i + 1] + line[i]
-        )
-        parts = [difference[g * 8 : g * 8 + 8] for g in range(NF)]
-        residual = []
-        for f in range(NF):
-            central = jac[f, 0] * parts[0]
-            for g in range(1, NF):
-                central += jac[f, g] * parts[g]
-            residual.append(smooth[f * 8 : f * 8 + 8] - 0.5 * central)
-        fields = []
-        for f in range(NF):
-            value = left[f, 0] * residual[0]
-            for g in range(1, NF):
-                value += left[f, g] * residual[g]
-            fields.append(value)
-        characteristic.append(jnp.concatenate(fields, axis=0))
-    for b, packed in enumerate(swap_blocks(characteristic)):
-        for f in range(NF):
-            low_s[pl.ds(b * 16 + 10 + f, 8, stride=64), :] = packed[f * 8 : f * 8 + 8]
-
-    def body_low(k, carry):
-        t = peer(k)
-        remote(
-            low_s.at[pl.ds(pl.multiple_of(t * 16, 16), 15)],
-            low_r.at[pl.ds(pl.multiple_of(s * 16, 16), 15)], 3, (t, c),
-        ).start()
-        return carry
-
-    lax.fori_loop(0, NS - 1, body_low, 0)
-    low_r[mine, :] = low_s[mine, :]
+        smooth = cell(src, 0, i) + dissipation * (line[i + 2] - 2.0 * line[i + 1] + line[i])
+        residual = smooth - 0.5 * mixed(jac, line[i + 2] - line[i])
+        rhs.append(mixed(left, residual) * inverse[i])
+    pack(low_s, 0, [sub2[3] * diag[1], rhs[1], rhs[2], rhs[0]])
+    pack(low_s, 5, [sub1[0] * diag1, sub2[0] * diag2, sub2[1] * diag1, rhs[3]])
+    to_owners(3, low_s, low_r, 10)
 
     loads[4].wait()
     loads[5].wait()
@@ -268,9 +262,9 @@
         sent.append(copy)
 
     arrived(2, up_s, up_r, (NS - 1) * 15, (after, c))
-    inverse = [1.0 / d for d in unpack(up_r, 0)]
-    alpha = [u * d for u, d in zip(unpack(up_r, 1), inverse)]
-    beta = [u * d for u, d in zip(unpack(up_r, 2), inverse)]
+    alpha, beta = unpack(up_r, 0), unpack(up_r, 1)
+    sub1, sub2 = [None] * 4, [None] * 4
+    sub1[1], sub1[2], sub1[3], sub2[2] = unpack(up_r, 2)
     bp, bq = [None] * 4, [None] * 4
     bp[3], bq[3] = -alpha[3], -beta[3]
     bp[2], bq[2] = -alpha[2] * bp[3] - beta[2], -alpha[2] * bq[3]
@@ -281,8 +275,10 @@
     b_mats = (bp[0], bq[0], bp[1], bq[1])
     b_one, b_two, b_before = prefix_mats(b_mats, b_shifts, b_edges)
 
-    arrived(3, low_s, low_r, (NS - 1) * 15, (after, c))
-    sub1, sub2, rhs = unpack(low_r, 0), unpack(low_r, 1), unpack(low_r, 2)
+    arrived(3, low_s, low_r, (NS - 1) * 10, (after, c))
+    rhs = [None] * 4
+    sub2[3], rhs[1], rhs[2], rhs[0] = unpack(low_r, 0)
+    sub1[0], sub2[0], sub2[1], rhs[3] = unpack(low_r, 1)
     fp, fq, fr = [-sub1[0]], [-sub2[0]], [rhs[0]]
     fp.append(-sub1[1] * fp[0] - sub2[1])
     fq.append(-sub1[1] * fq[0])
@@ -297,7 +293,7 @@
     f_vecs, f_vecs_before = prefix_vecs(f_mats, f_one, (fr[3], fr[2]), f_shifts, f_edges)
     state = walk(f_two, f_vecs, list(range(8)), 3)
     enter = entering(f_before, f_vecs_before, state)
-    gamma = [(fp[i] * enter[0] + fq[i] * enter[1] + fr[i]) * inverse[i] for i in range(4)]
+    gamma = [fp[i] * enter[0] + fq[i] * enter[1] + fr[i] for i in range(4)]
 
     br = [None] * 4
     br[3] = gamma[3]
@@ -309,18 +305,9 @@
     enter = entering(b_before, b_vecs_before, state)
     solved = [bp[i] * enter[0] + bq[i] * enter[1] + br[i] for i in range(4)]
 
-    increment = []
-    squares = jnp.zeros((8, 128), F32)
-    for i in range(4):
-        parts = [solved[i][g * 8 : g * 8 + 8] for g in range(NF)]
-        fields = []
-        for f in range(NF):
-            value = right[f, 0] * parts[0]
-            for g in range(1, NF):
-                value += right[f, g] * parts[g]
-            squares += value * value
-            fields.append(value)
-        increment.append(jnp.concatenate(fields, axis=0))
+    increment = [mixed(right, entry) for entry in solved]
+    squares = sum(entry * entry for entry in increment)
+    squares = sum(squares[f * 8 : f * 8 + 8] for f in range(NF))
 
     sq_s[...] = jnp.broadcast_to(jnp.sum(squares, axis=0, keepdims=True), (8, 128))
     one_row = pl.ds(0, 1)
@@ -412,8 +399,10 @@
             vmem((320, 128), F32),
             vmem((480, 128), F32),
             vmem((32, 128), jnp.int32),
-            vmem((2, 40, 128), F32),
-            vmem((2, 40, 128), F32),
+            vmem((120, 128), F32),
+            vmem((120, 128), F32),
+            vmem((40, 128), F32),
+            vmem((40, 128), F32),
             vmem((512, 128), F32),
             vmem((512, 128), F32),
             vmem((512, 128), F32),

time: 46 us -> 45.1 us (0.980)
  Pallas kernels: 43.1 us -> 42.1 us
    pallas_call x1, Pallas kernels: 43.1 us -> 42.1 us  [shards(): pl.pallas_call(kernel, out_shape=(jax.ShapeDtypeStruct((160, 128), F32),...]
where the time goes in v3:
time: 45.1 us; the launch traced here: 44.9 us
  Pallas kernels  42.1 us (93%)
  local copies, waits for them, and re-layouts  2.13 us (5%)
  between operations  0.65 us (1%)
    pallas_call x1, Pallas kernels, shards(): pl.pallas_call(kernel, out_shape=(jax.ShapeDtypeStruct((160, 128), F32),...  42.1 us
    unnamed x4, local copies, waits for them, and re-layouts  2.13 us

profile of v3, /device:TPU:1, one launch (start us, length us, event | category | flops | bytes accessed | tf_op | source)
XLA Modules:
  0.0 44.9 jit_solution(16207044860981411180)
XLA Ops:
  0.6 42.1 %shard_map.104 = (f32[160,128]{1,0:T(8,128)}, f32[8,128]{1,0:T(8,128)}) custom-call(f32[5,5]{1,0:T(8,128)} %jac_h.1, f32[5,5]{1,0:T(8,128)} %left_h.1, f32[5,5]{1,0:T(8,128)} %right_h.1, f32[160,128]{1,0:T(8,128)} %bitcast.39, f32[160,128]{1,0:T(8,128)} %bitcast.40, f32[160,128]{1,0:T(8,128)} %bitcast.41, f32[320,128]{1,0:T(8,128)} %bitcast.37, ...), custom_call_target="tpu_custom_call" | custom-call | tf_op jit(solution)/shard_map/pallas_call | solution.py:387
  42.7 0.0 copy-start
  42.8 1.5 %copy.20 = f32[5,4,1024]{2,1,0:T(4,128)} copy(f32[5,4,1024]{2,1,0:T(4,128)} %bitcast.38) | data formatting | bytes 163840
  44.3 0.0 copy-done
  44.3 0.6 %copy.21 = f32[1024]{0:T(1024)} copy(f32[1024]{0:T(1024)S(1)} %bitcast.43) | data formatting | bytes 8192
Async XLA Ops:
  42.7 1.5 %copy-start = (f32[8,128]{1,0:T(8,128)S(1)}, f32[8,128]{1,0:T(8,128)}, u32[]{:S(2)}) copy-start(f32[8,128]{1,0:T(8,128)} %get-tuple-element.5) | copy-start | bytes 12292

commit v4 on v3

--- a/solution.py
+++ b/solution.py
@@ -424,12 +424,13 @@
             pltpu.SemaphoreType.DMA((8,)),
         ],
         compiler_params=pltpu.CompilerParams(
-            collective_id=0, has_side_effects=True, vmem_limit_bytes=60 * 2**20
+            collective_id=0, has_side_effects=True, vmem_limit_bytes=40 * 2**20
         ),
     )(
+        *(pltpu.with_memory_space_constraint(x, pltpu.HBM) for x in (
         jacobian, left, right,
         rows_of(adjoint), rows_of(source), rows_of(shape_grad), rows_of(lower_band),
-        rows_of(upper_band), rows_of(ctrl_local),
+        rows_of(upper_band), rows_of(ctrl_local)))
     )
     adjoint_next = jnp.swapaxes(out.reshape(NF, 8, 4, 128), 1, 2).reshape(NF, 4, 1024)
     return adjoint_next, sens.reshape(1024)

time: 45.1 us -> 43.5 us (0.965)
  local copies, waits for them, and re-layouts: 2.13 us -> 1.23 us
  Pallas kernels: 42.1 us -> 41.5 us
    unnamed x4 -> x2, local copies, waits for them, and re-layouts: 2.13 us -> 1.23 us
    pallas_call x1, Pallas kernels: 42.1 us -> 41.5 us  [shards(): pl.pallas_call(kernel, out_shape=(jax.ShapeDtypeStruct((160, 128), F32),...]
where the time goes in v4:
time: 43.5 us; the launch traced here: 43.4 us
  Pallas kernels  41.5 us (95%)
  local copies, waits for them, and re-layouts  1.23 us (3%)
  between operations  0.64 us (1%)
    pallas_call x1, Pallas kernels, shards(): pl.pallas_call(kernel, out_shape=(jax.ShapeDtypeStruct((160, 128), F32),...  41.5 us
    unnamed x2, local copies, waits for them, and re-layouts  1.23 us

profile of v4, /device:TPU:1, one launch (start us, length us, event | category | flops | bytes accessed | tf_op | source)
XLA Modules:
  0.0 43.4 jit_solution(5890271670339760015)
XLA Ops:
  0.6 41.5 %shard_map.104 = (f32[160,128]{1,0:T(8,128)S(1)}, f32[8,128]{1,0:T(8,128)S(1)}) custom-call(f32[5,5]{1,0:T(8,128)} %jac_h.1, f32[5,5]{1,0:T(8,128)} %left_h.1, f32[5,5]{1,0:T(8,128)} %right_h.1, f32[160,128]{1,0:T(8,128)} %bitcast.40, f32[160,128]{1,0:T(8,128)} %bitcast.41, f32[160,128]{1,0:T(8,128)} %bitcast.42, f32[320,128]{1,0:T(8,128)} %bitcast.39, ...), custom_call_target="tpu_custom_call" | custom-call | tf_op jit(solution)/shard_map/pallas_call | solution.py:387
  42.1 0.6 %copy.20 = f32[5,4,1024]{2,1,0:T(4,128)} copy(f32[5,4,1024]{2,1,0:T(4,128)S(1)} %bitcast.36) | data formatting | bytes 163840
  42.8 0.6 %copy.21 = f32[1024]{0:T(1024)} copy(f32[1024]{0:T(1024)S(1)} %bitcast.37) | data formatting | bytes 8192

commit v5 on v4

--- a/solution.py
+++ b/solution.py
@@ -142,11 +142,23 @@
         up_s, 10, [sub1[1] * diag[0], sub1[2] * diag[1], sub1[3] * diag[2], sub2[2] * diag[0]]
     )
 
+    for n in (3, 6, 7, 8):
+        loads[n].wait()
+    zero = jnp.zeros((40, 128), F32)
+    line = [zero] + own + [zero]
+    rhs = []
+    for i in range(4):
+        smooth = cell(src, 0, i) + dissipation * (line[i + 2] - 2.0 * line[i + 1] + line[i])
+        residual = smooth - 0.5 * mixed(jac, line[i + 2] - line[i])
+        rhs.append(mixed(left, residual) * inverse[i])
+
     pl.semaphore_wait(barrier, NS - 1 + NC - 1)
-    behind_copy = remote(next_s, next_r, 0, (after, c))
+    behind_copies = [remote(next_s.at[pl.ds(i * 40, 40)], next_r.at[pl.ds(i * 40, 40)], (0, 8, 9)[i], (after, c)) for i in range(3)]
     ahead_copy = remote(last_s, last_r, 1, (before, c))
-    behind_copy.start()
+    behind_copies[0].start()
     ahead_copy.start()
+    behind_copies[1].start()
+    behind_copies[2].start()
 
     def to_owners(n, source, dest, rows):
         def body(k, carry):
@@ -163,21 +175,17 @@
 
     to_owners(2, up_s, up_r, 15)
 
-    for n in (3, 6, 7, 8):
-        loads[n].wait()
-    behind_copy.wait_recv()
+    behind_copies[0].wait_recv()
     ahead_copy.wait_recv()
-    sent += [behind_copy, ahead_copy]
     first = jnp.where(s == 0, 0.0, next_r[0:40])
     last = jnp.where(s == NS - 1, 0.0, last_r[...])
+    rhs[0] += mixed(left, 0.5 * mixed(jac, first) + dissipation * first) * inverse[0]
+    rhs[3] += mixed(left, dissipation * last - 0.5 * mixed(jac, last)) * inverse[3]
+    pack(low_s, 0, [sub2[3] * diag[1], rhs[1], rhs[2], rhs[0]])
+    behind_copies[1].wait_recv()
+    behind_copies[2].wait_recv()
+    sent += [*behind_copies, ahead_copy]
     diag1, diag2 = next_r[40:80], next_r[80:120]
-    line = [first] + own + [last]
-    rhs = []
-    for i in range(4):
-        smooth = cell(src, 0, i) + dissipation * (line[i + 2] - 2.0 * line[i + 1] + line[i])
-        residual = smooth - 0.5 * mixed(jac, line[i + 2] - line[i])
-        rhs.append(mixed(left, residual) * inverse[i])
-    pack(low_s, 0, [sub2[3] * diag[1], rhs[1], rhs[2], rhs[0]])
     pack(low_s, 5, [sub1[0] * diag1, sub2[0] * diag2, sub2[1] * diag1, rhs[3]])
     to_owners(3, low_s, low_r, 10)
 
@@ -313,12 +321,12 @@
     one_row = pl.ds(0, 1)
 
     def body_sq(k, carry):
-        t = peer(k)
-        remote(sq_s.at[one_row], sq_r.at[s, one_row], 5, (t, c)).start()
+        t = cross_peer(k)
+        remote(sq_s.at[one_row], sq_r.at[c, one_row], 5, (s, t)).start()
         return carry
 
-    lax.fori_loop(0, NS - 1, body_sq, 0)
-    sq_r[s] = sq_s[...]
+    lax.fori_loop(0, NC - 1, body_sq, 0)
+    sq_r[c] = sq_s[...]
 
     for x, packed in enumerate(swap_blocks(increment)):
         for f in range(NF):
@@ -341,18 +349,18 @@
         copy.wait_recv()
         sent.append(copy)
 
-    rows_arrived(5, sq_r, NS - 1, (after, c))
+    rows_arrived(5, sq_r, NC - 1, (s, (c + 1) % NC))
     sq2_s[...] = jnp.broadcast_to(
         jnp.sum(sq_r[:, 0, :], axis=0, keepdims=True), (8, 128)
     )
 
     def body_sq2(k, carry):
-        t = cross_peer(k)
-        remote(sq2_s.at[one_row], sq2_r.at[c, one_row], 7, (s, t)).start()
+        t = peer(k)
+        remote(sq2_s.at[one_row], sq2_r.at[s, one_row], 7, (t, c)).start()
         return carry
 
-    lax.fori_loop(0, NC - 1, body_sq2, 0)
-    sq2_r[c] = sq2_s[...]
+    lax.fori_loop(0, NS - 1, body_sq2, 0)
+    sq2_r[s] = sq2_s[...]
 
     arrived(4, sums, cross_r, NC - 1, (s, (c + 1) % NC))
     sens[...] = jnp.sum(cross_r[...], axis=0)
@@ -366,7 +374,7 @@
     ]
     mine_inc = swap_blocks(per_b)
 
-    rows_arrived(7, sq2_r, NC - 1, (s, (c + 1) % NC))
+    rows_arrived(7, sq2_r, NS - 1, (after, c))
     total = jnp.sum(jnp.sum(sq2_r[:, 0, :], axis=0, keepdims=True), axis=1, keepdims=True)
     scale = step_scale / jnp.sqrt(total * (1.0 / CELLS) + epsilon)
     for i in range(4):
@@ -414,14 +422,14 @@
             vmem((16, 8, 128), F32),
             vmem((16, 8, 128), F32),
             vmem((8, 128), F32),
+            vmem((16, 8, 128), F32),
+            vmem((8, 128), F32),
             vmem((32, 8, 128), F32),
-            vmem((8, 128), F32),
-            vmem((16, 8, 128), F32),
             vmem((6, 40, 128), F32),
             vmem((2, 40, 128), F32),
             pltpu.SemaphoreType.DMA((9,)),
-            pltpu.SemaphoreType.DMA((8,)),
-            pltpu.SemaphoreType.DMA((8,)),
+            pltpu.SemaphoreType.DMA((10,)),
+            pltpu.SemaphoreType.DMA((10,)),
         ],
         compiler_params=pltpu.CompilerParams(
             collective_id=0, has_side_effects=True, vmem_limit_bytes=40 * 2**20

time: 43.5 us -> 42.6 us (0.979)
  Pallas kernels: 41.5 us -> 40.6 us
    pallas_call x1, Pallas kernels: 41.5 us -> 40.6 us  [shards(): pl.pallas_call(kernel, out_shape=(jax.ShapeDtypeStruct((160, 128), F32),...]
where the time goes in v5:
time: 42.6 us; the launch traced here: 42.4 us
  Pallas kernels  40.6 us (95%)
  local copies, waits for them, and re-layouts  1.23 us (3%)
  between operations  0.64 us (2%)
    pallas_call x1, Pallas kernels, shards(): pl.pallas_call(kernel, out_shape=(jax.ShapeDtypeStruct((160, 128), F32),...  40.6 us
    unnamed x2, local copies, waits for them, and re-layouts  1.23 us

profile of v5, /device:TPU:1, one launch (start us, length us, event | category | flops | bytes accessed | tf_op | source)
XLA Modules:
  0.0 42.4 jit_solution(3433010988725650451)
XLA Ops:
  0.6 40.6 %shard_map.104 = (f32[160,128]{1,0:T(8,128)S(1)}, f32[8,128]{1,0:T(8,128)S(1)}) custom-call(f32[5,5]{1,0:T(8,128)} %jac_h.1, f32[5,5]{1,0:T(8,128)} %left_h.1, f32[5,5]{1,0:T(8,128)} %right_h.1, f32[160,128]{1,0:T(8,128)} %bitcast.40, f32[160,128]{1,0:T(8,128)} %bitcast.41, f32[160,128]{1,0:T(8,128)} %bitcast.42, f32[320,128]{1,0:T(8,128)} %bitcast.39, ...), custom_call_target="tpu_custom_call" | custom-call | tf_op jit(solution)/shard_map/pallas_call | solution.py:395
  41.2 0.6 %copy.20 = f32[5,4,1024]{2,1,0:T(4,128)} copy(f32[5,4,1024]{2,1,0:T(4,128)S(1)} %bitcast.36) | data formatting | bytes 163840
  41.8 0.6 %copy.21 = f32[1024]{0:T(1024)} copy(f32[1024]{0:T(1024)S(1)} %bitcast.37) | data formatting | bytes 8192

commit v6 on v5

--- a/solution.py
+++ b/solution.py
@@ -335,8 +335,8 @@
     def body_inc(k, carry):
         t = peer(k)
         remote(
-            inc_s.at[pl.ds(pl.multiple_of(t * 8, 8), 8)],
-            inc_r.at[pl.ds(pl.multiple_of(s * 8, 8), 8)], 6, (t, c),
+            inc_s.at[pl.ds(pl.multiple_of(t * 8, 8), NF)],
+            inc_r.at[pl.ds(pl.multiple_of(s * 8, 8), NF)], 6, (t, c),
         ).start()
         return carry
 
@@ -365,7 +365,7 @@
     arrived(4, sums, cross_r, NC - 1, (s, (c + 1) % NC))
     sens[...] = jnp.sum(cross_r[...], axis=0)
 
-    arrived(6, inc_s, inc_r, (NS - 1) * 8, (after, c))
+    arrived(6, inc_s, inc_r, (NS - 1) * NF, (after, c))
     per_b = [
         jnp.concatenate(
             [inc_r[pl.ds(b * 8 + f, 8, stride=32), :] for f in range(NF)], axis=0

time: 42.6 us -> 42.6 us (level)
  no operation moved by 1% of the time
where the time goes in v6:
time: 42.6 us; the launch traced here: 42.4 us
  Pallas kernels  40.6 us (95%)
  local copies, waits for them, and re-layouts  1.23 us (3%)
  between operations  0.64 us (2%)
    pallas_call x1, Pallas kernels, shards(): pl.pallas_call(kernel, out_shape=(jax.ShapeDtypeStruct((160, 128), F32),...  40.6 us
    unnamed x2, local copies, waits for them, and re-layouts  1.23 us

profile of v6, /device:TPU:1, one launch (start us, length us, event | category | flops | bytes accessed | tf_op | source)
XLA Modules:
  0.0 42.4 jit_solution(11257946973542162491)
XLA Ops:
  0.6 40.6 %shard_map.104 = (f32[160,128]{1,0:T(8,128)S(1)}, f32[8,128]{1,0:T(8,128)S(1)}) custom-call(f32[5,5]{1,0:T(8,128)} %jac_h.1, f32[5,5]{1,0:T(8,128)} %left_h.1, f32[5,5]{1,0:T(8,128)} %right_h.1, f32[160,128]{1,0:T(8,128)} %bitcast.40, f32[160,128]{1,0:T(8,128)} %bitcast.41, f32[160,128]{1,0:T(8,128)} %bitcast.42, f32[320,128]{1,0:T(8,128)} %bitcast.39, ...), custom_call_target="tpu_custom_call" | custom-call | tf_op jit(solution)/shard_map/pallas_call | solution.py:395
  41.2 0.6 %copy.20 = f32[5,4,1024]{2,1,0:T(4,128)} copy(f32[5,4,1024]{2,1,0:T(4,128)S(1)} %bitcast.36) | data formatting | bytes 163840
  41.8 0.6 %copy.21 = f32[1024]{0:T(1024)} copy(f32[1024]{0:T(1024)S(1)} %bitcast.37) | data formatting | bytes 8192

commit v7 on v6

--- a/solution.py
+++ b/solution.py
@@ -57,7 +57,7 @@
     s, c = lax.axis_index("stream"), lax.axis_index("cross")
 
     def peer(k):
-        m, n = k // 4, k % 4
+        m, n = k % 8, k // 8
         z = (s // 4 + 4 + (m + 1) // 2 * (1 - 2 * (m % 2))) % 8
         x = (s % 4 + 2 + (n + 1) // 2 * (1 - 2 * (n % 2))) % 4
         return z * 4 + x

time: 42.6 us -> 43.2 us (1.014)
  Pallas kernels: 40.6 us -> 41.2 us
    pallas_call x1, Pallas kernels: 40.6 us -> 41.2 us  [shards(): pl.pallas_call(kernel, out_shape=(jax.ShapeDtypeStruct((160, 128), F32),...]
where the time goes in v7:
time: 43.2 us; the launch traced here: 43.1 us
  Pallas kernels  41.2 us (95%)
  local copies, waits for them, and re-layouts  1.23 us (3%)
  between operations  0.64 us (1%)
    pallas_call x1, Pallas kernels, shards(): pl.pallas_call(kernel, out_shape=(jax.ShapeDtypeStruct((160, 128), F32),...  41.2 us
    unnamed x2, local copies, waits for them, and re-layouts  1.23 us

profile of v7, /device:TPU:1, one launch (start us, length us, event | category | flops | bytes accessed | tf_op | source)
XLA Modules:
  0.0 43.1 jit_solution(8729161449639543198)
XLA Ops:
  0.6 41.2 %shard_map.104 = (f32[160,128]{1,0:T(8,128)S(1)}, f32[8,128]{1,0:T(8,128)S(1)}) custom-call(f32[5,5]{1,0:T(8,128)} %jac_h.1, f32[5,5]{1,0:T(8,128)} %left_h.1, f32[5,5]{1,0:T(8,128)} %right_h.1, f32[160,128]{1,0:T(8,128)} %bitcast.40, f32[160,128]{1,0:T(8,128)} %bitcast.41, f32[160,128]{1,0:T(8,128)} %bitcast.42, f32[320,128]{1,0:T(8,128)} %bitcast.39, ...), custom_call_target="tpu_custom_call" | custom-call | tf_op jit(solution)/shard_map/pallas_call | solution.py:395
  41.8 0.6 %copy.20 = f32[5,4,1024]{2,1,0:T(4,128)} copy(f32[5,4,1024]{2,1,0:T(4,128)S(1)} %bitcast.36) | data formatting | bytes 163840
  42.5 0.6 %copy.21 = f32[1024]{0:T(1024)} copy(f32[1024]{0:T(1024)S(1)} %bitcast.37) | data formatting | bytes 8192
